TPU v7x, 256 devices: a whole 4x4x8 slice. The times are simulated.
256 devices in a mesh: row: 32 (over z, x), col: 8 (over y, core).
Axes of the slice: x: 4, y: 4, z: 8, core: 2. Of those that a mesh axis runs over, the one named last changes fastest.
Arguments:
- vectors: bfloat16 [256, 65536], P('col', 'row'), may hold values from -6 to 6
- hblocks: bfloat16 [1024, 12, 4096], P('row'), may hold values from -0.15625 to 0.15625
- counts: int32 [1024], P('row'), may hold values from 3 to 12, as said below
- sources: int32 [1024, 12], P('row'), may hold values from 0 to 95, as said below
- send_rows: int32 [2048], P('row'), may hold values from 0 to 31
Outputs:
- filtered: bfloat16 [256, 65536], P('col', 'row')
- gram_matrix: float32 [256, 256], P(None, 'col')
- projected: float32 [256, 256], P(None, 'col')
Inputs may be any that keep to these rules, and one draw needn't show every extreme that they name: Blocks 0 to counts[i] - 1 of block row i are live; the rows of every device include one with 12 live blocks. `sources`: entry 0 of block row i is i's own index within its device. On every device each slot value 32 + s, s below 64, stands exactly once, at block 1 or 2 of some row. `send_rows`: entries p * 64 + q * 2 + c name block rows of device p within it.
All inputs are finite; a program needn't handle non-finite values.
Results may differ from a plain program's by a relative error of at most 0.017.
Values may be sent and summed in bfloat16 or wider, within the bound.
No kernel may reach another device: no remote copies, remote signals or barrier semaphores. Data moves between devices by JAX's collectives and lax.ppermute only.
A program may use at most 128 MiB of HBM per device.

v0:
```python
import jax
import jax.numpy as jnp
from jax import lax
from jax.sharding import PartitionSpec as P

B = 64
K = 12
center_value = 0.25
half_width = 1.5


def on_device(vectors, hblocks, counts, sources, send_rows):
    rows_here = hblocks.shape[0]
    cols_here = vectors.shape[0]
    slots = send_rows.shape[0]
    live_mask = lax.broadcasted_iota(jnp.int32, (rows_here, K), 1) < counts[:, None]
    masked = jnp.where(live_mask[:, :, None], hblocks, jnp.zeros((), jnp.bfloat16)).reshape(
        rows_here, K, B, B
    )
    flat_sources = sources.reshape(-1)
    slot_table = lax.all_gather(send_rows, "row", axis=0, tiled=True)
    device_row = lax.axis_index("row")
    capacity = slots // lax.axis_size("row")
    positions = jnp.arange(slots, dtype=jnp.int32)
    peer_index = positions // capacity
    global_rows = (
        peer_index * rows_here
        + slot_table[peer_index * slots + device_row * capacity + positions % capacity]
    )

    def apply_operator(block_vectors):
        whole_blocks = lax.all_gather(block_vectors, "row", axis=0, tiled=True)
        incoming = whole_blocks[global_rows]
        extended = jnp.concatenate([block_vectors, incoming], 0)
        picked = extended[flat_sources].reshape(rows_here, K, cols_here, B)
        upper_part = jnp.einsum(
            "ikmb,ikab->ima", picked, masked, preferred_element_type=jnp.float32
        )
        mirror = jnp.einsum(
            "ima,ikab->ikmb", block_vectors, masked, preferred_element_type=jnp.float32
        )
        spread = jax.ops.segment_sum(
            mirror.reshape(rows_here * K, cols_here, B),
            flat_sources,
            num_segments=rows_here + slots,
        )
        returned = lax.all_to_all(
            spread[rows_here:], "row", split_axis=0, concat_axis=0, tiled=True
        )
        back_sums = jax.ops.segment_sum(returned, send_rows, num_segments=rows_here)
        return upper_part + spread[:rows_here] + back_sums

    start_blocks = vectors.reshape(cols_here, rows_here, B).transpose(1, 0, 2)
    start_float = start_blocks.astype(jnp.float32)
    first_image = apply_operator(start_blocks)
    first_step = ((first_image - center_value * start_float) / half_width).astype(jnp.bfloat16)
    second_image = apply_operator(first_step)
    second_step = (
        2.0 * (second_image - center_value * first_step.astype(jnp.float32)) / half_width
        - start_float
    ).astype(jnp.bfloat16)
    image_blocks = apply_operator(second_step).astype(jnp.bfloat16)
    filtered = second_step.transpose(1, 0, 2).reshape(cols_here, rows_here * B)
    image_rows = image_blocks.transpose(1, 0, 2).reshape(cols_here, rows_here * B)
    contract = (((1,), (1,)), ((), ()))
    stacked = jnp.concatenate([filtered, image_rows], 0)
    partial_value = lax.dot_general(
        lax.all_gather(filtered, "col", axis=0, tiled=True),
        stacked,
        contract,
        preferred_element_type=jnp.float32,
    )
    partial_value = partial_value.reshape(partial_value.shape[0], 2, cols_here)
    totals = lax.psum(partial_value.astype(jnp.bfloat16), "row").astype(jnp.float32)
    return (filtered, totals[:, 0, :], totals[:, 1, :])


def solution(mesh):
    return jax.shard_map(
        on_device,
        mesh=mesh,
        in_specs=(P("col", "row"), P("row", None, None), P("row"), P("row", None), P("row")),
        out_specs=(P("col", "row"), P(None, "col"), P(None, "col")),
        check_vma=False,
    )
```

profile of v0, /device:TPU:16, one launch (start us, length us, event | category | flops | bytes accessed | tf_op | source)
XLA Modules:
  0.0 545.5 jit_solution(17651293404976288670)
XLA Ops:
  7.2 1.2 reshape.175
  8.4 0.8 copy.75
  10.7 2.2 broadcast_select_fusion
  12.8 7.9 %reshape.178 = bf16[32,12,64,64]{3,2,0,1:T(8,128)(2,1)} reshape(bf16[32,12,4096]{2,0,1:T(8,128)(2,1)S(1)} %broadcast_select_fusion) | data formatting | bytes 6291456 | tf_op jit(solution)/shard_map/reshape | solution.py:17
  20.8 6.4 %fusion = f32[32,12,64,32]{2,3,1,0:T(8,128)} fusion(bf16[32,12,64,64]{3,2,0,1:T(8,128)(2,1)} %reshape.178, bf16[32,32,64]{2,1,0:T(8,128)(2,1)S(1)} %reshape.175), kind=kOutput, calls=%fused_computation.14 | convolution fusion | flops 100663296 | bytes 6422528 | tf_op jit(solution)/shard_map/ima,ikab->ikmb/dot_general | solution.py:39
  27.4 34.4 %scatter_fusion = f32[96,32,64]{2,1,0:T(8,128)S(1)} fusion(f32[96,32,64]{2,1,0:T(8,128)S(1)} %broadcast.194.clone, s32[384]{0:T(512)S(1)} %reshape.244, f32[384,32,64]{2,1,0:T(8,128)} %bitcast.74), kind=kCustom, calls=%fused_computation.7 | custom fusion | flops 786432 | bytes 9438720 | tf_op jit(solution)/shard_map/scatter-add | solution.py:42
  61.9 1.5 reshape.308
  63.3 11.3 %all-to-all-start = ((f32[32,1,4096]{2,1,0:T(1,128)}), f32[32,1,4096]{2,1,0:T(1,128)S(1)}, u32[]{:S(2)}, u32[]{:S(2)}) async-start(f32[32,1,4096]{2,1,0:T(1,128)} %reshape.308), calls=%async_computation | async-start | bytes 1048576 | tf_op jit(solution)/shard_map/all_to_all | solution.py:47
  76.3 26.1 %all-reduce = s32[2048]{0:T(1024)S(1)} all-reduce(s32[2048]{0:T(1024)S(1)} %dynamic-update-slice), channel_id=1, replica_groups=mesh['row'=32,'col'=8] {'row'}, use_global_device_ids=true, to_apply=%add | all-reduce | flops 2048 | bytes 16384
  103.8 1.9 reduce.2
  105.7 1.4 reshape.309
  107.1 13.4 %all-gather.5.cloned.1.call-done = bf16[1024,32,64]{2,1,0:T(8,128)(2,1)} async-done(((bf16[32,32,64]{2,1,0:T(8,128)(2,1)}), bf16[1024,32,64]{2,1,0:T(8,128)(2,1)}) %all-gather.5.cloned.1.call-update) | async-done | bytes 4194320 | tf_op jit(solution)/shard_map/all_gather | solution.py:32
  120.5 4.8 gather_fusion.1
  125.3 1.2 pad_maximum_fusion
  126.5 3.2 gather_fusion.2
  129.7 5.6 %fusion.27 = f32[32,32,64]{2,1,0:T(8,128)S(1)} fusion(bf16[32,12,32,64]{3,2,1,0:T(8,128)(2,1)} %bitcast.78, bf16[32,12,64,64]{3,2,0,1:T(8,128)(2,1)} %reshape.178, f32[96,32,64]{2,1,0:T(8,128)S(1)} %scatter_fusion), kind=kOutput, calls=%fused_computation.31 | convolution fusion | flops 100728832 | bytes 5242880 | tf_op jit(solution)/shard_map/ikmb,ikab->ima/dot_general | solution.py:36
  135.3 3.2 scatter_fusion.1
  138.4 0.8 fusion.32
  139.5 6.4 %fusion.4 = f32[32,12,64,32]{2,3,1,0:T(8,128)} fusion(bf16[32,12,64,64]{3,2,0,1:T(8,128)(2,1)} %reshape.178, bf16[32,32,64]{2,1,0:T(8,128)(2,1)} %fusion.32), kind=kOutput, calls=%fused_computation.18 | convolution fusion | flops 100663296 | bytes 6422528 | tf_op jit(solution)/shard_map/ima,ikab->ikmb/dot_general | solution.py:39
  146.1 34.4 %scatter_fusion.2 = f32[96,32,64]{2,1,0:T(8,128)S(1)} fusion(f32[96,32,64]{2,1,0:T(8,128)S(1)} %broadcast.194.clone.1, s32[384]{0:T(512)S(1)} %reshape.244, f32[384,32,64]{2,1,0:T(8,128)} %bitcast.75), kind=kCustom, calls=%fused_computation.9 | custom fusion | flops 786432 | bytes 9438720 | tf_op jit(solution)/shard_map/scatter-add | solution.py:42
  180.6 1.0 slice.49
  181.6 1.9 reshape.310
  183.5 30.1 %all_to_all.15 = f32[32,1,4096]{2,1,0:T(1,128)S(1)} all-to-all(f32[32,1,4096]{2,1,0:T(1,128)S(1)} %reshape.310), channel_id=1, replica_groups=mesh['row'=32,'col'=8] {'row'}, dimensions={0} | all-to-all | bytes 1048576 | tf_op jit(solution)/shard_map/all_to_all | solution.py:47
  213.6 1.9 reduce.3
  215.5 1.4 reshape.311
  216.9 26.6 %all-gather.7.cloned.1.call-done = bf16[1024,32,64]{2,1,0:T(8,128)(2,1)} async-done(((bf16[32,32,64]{2,1,0:T(8,128)(2,1)}), bf16[1024,32,64]{2,1,0:T(8,128)(2,1)}) %all-gather.7.cloned.1.call-update) | async-done | bytes 4194320 | tf_op jit(solution)/shard_map/all_gather | solution.py:32
  243.5 4.0 gather_fusion.3
  247.8 3.2 gather_fusion.4
  250.9 5.5 %fusion.24 = f32[32,32,64]{2,1,0:T(8,128)S(1)} fusion(bf16[32,12,32,64]{3,2,1,0:T(8,128)(2,1)} %bitcast.79, bf16[32,12,64,64]{3,2,0,1:T(8,128)(2,1)} %reshape.178, f32[96,32,64]{2,1,0:T(8,128)S(1)} %scatter_fusion.2), kind=kOutput, calls=%fused_computation.30 | convolution fusion | flops 100728832 | bytes 5242880 | tf_op jit(solution)/shard_map/ikmb,ikab->ima/dot_general | solution.py:36
  256.4 6.1 %scatter_fusion.3 = f32[32,32,64]{2,1,0:T(8,128)S(1)} fusion(f32[32,32,64]{2,1,0:T(8,128)S(1)} %fusion.24, s32[64]{0:T(128)S(1)} %copy-done.6, f32[64,32,64]{2,1,0:T(8,128)} %reshape.311), kind=kCustom, calls=%fused_computation.10 | custom fusion | flops 131072 | bytes 1573120 | tf_op jit(solution)/shard_map/scatter-add | solution.py:50
  262.6 0.9 fusion.33
  263.5 6.4 %fusion.8 = f32[32,12,64,32]{2,3,1,0:T(8,128)} fusion(bf16[32,12,64,64]{3,2,0,1:T(8,128)(2,1)} %reshape.178, bf16[32,32,64]{2,1,0:T(8,128)(2,1)} %fusion.33), kind=kOutput, calls=%fused_computation.22 | convolution fusion | flops 100663296 | bytes 6422528 | tf_op jit(solution)/shard_map/ima,ikab->ikmb/dot_general | solution.py:39
  270.1 34.4 %scatter_fusion.4 = f32[96,32,64]{2,1,0:T(8,128)S(1)} fusion(f32[96,32,64]{2,1,0:T(8,128)S(1)} %broadcast.194, s32[384]{0:T(512)S(1)} %reshape.244, f32[384,32,64]{2,1,0:T(8,128)} %bitcast.73), kind=kCustom, calls=%fused_computation.11 | custom fusion | flops 786432 | bytes 9438720 | tf_op jit(solution)/shard_map/scatter-add | solution.py:42
  304.5 1.0 slice.51
  305.5 2.7 reshape.312
  308.2 7.1 %all-to-all-start.2 = ((f32[32,1,4096]{2,1,0:T(1,128)}), f32[32,1,4096]{2,1,0:T(1,128)S(1)}, u32[]{:S(2)}, u32[]{:S(2)}) async-start(f32[32,1,4096]{2,1,0:T(1,128)} %reshape.312), calls=%async_computation.2 | async-start | bytes 1048576 | tf_op jit(solution)/shard_map/all_to_all | solution.py:47
  315.7 0.9 reshape.182
  316.7 22.2 %all-to-all-done.2 = f32[32,1,4096]{2,1,0:T(1,128)S(1)} async-done(((f32[32,1,4096]{2,1,0:T(1,128)}), f32[32,1,4096]{2,1,0:T(1,128)S(1)}, u32[]{:S(2)}, u32[]{:S(2)}) %all-to-all-start.2) | async-done | bytes 524320 | tf_op jit(solution)/shard_map/all_to_all | solution.py:47
  338.9 1.9 reduce.4
  340.8 1.4 reshape.313
  342.2 25.9 %all-gather.11.cloned.1.call-done = bf16[1024,32,64]{2,1,0:T(8,128)(2,1)} async-done(((bf16[32,32,64]{2,1,0:T(8,128)(2,1)}), bf16[1024,32,64]{2,1,0:T(8,128)(2,1)}) %all-gather.11.cloned.1.call-update) | async-done | bytes 4194320 | tf_op jit(solution)/shard_map/all_gather | solution.py:32
  368.1 4.0 gather_fusion.5
  372.3 3.2 gather_fusion.6
  375.5 5.6 %fusion.21 = f32[32,32,64]{2,1,0:T(8,128)S(1)} fusion(bf16[32,12,32,64]{3,2,1,0:T(8,128)(2,1)} %bitcast.77, bf16[32,12,64,64]{3,2,0,1:T(8,128)(2,1)} %reshape.178, f32[96,32,64]{2,1,0:T(8,128)S(1)} %scatter_fusion.4), kind=kOutput, calls=%fused_computation.29 | convolution fusion | flops 100728832 | bytes 5242880 | tf_op jit(solution)/shard_map/ikmb,ikab->ima/dot_general | solution.py:36
  381.1 3.2 scatter_fusion.5
  384.7 8.9 %all-gather.9.cloned.1.call-done = bf16[256,2048]{1,0:T(8,128)(2,1)} async-done(((bf16[32,2048]{1,0:T(8,128)(2,1)}), bf16[256,2048]{1,0:T(8,128)(2,1)}) %all-gather.9.cloned.1.call-update) | async-done | bytes 1048592 | tf_op jit(solution)/shard_map/all_gather | solution.py:68
  393.6 1.7 convolution_convert_fusion
  395.2 143.1 %psum.7 = bf16[256,2,32]{0,2,1:T(8,128)(2,1)S(1)} all-reduce(bf16[256,2,32]{0,2,1:T(8,128)(2,1)S(1)} %bitcast.82), channel_id=1, replica_groups=mesh['row'=32,'col'=8] {'row'}, use_global_device_ids=true, to_apply=%region_6.7 | all-reduce | flops 16384 | bytes 65536 | tf_op jit(solution)/shard_map/psum | solution.py:74
  (52 shorter events, 6.6 us)
Async XLA Ops:
  7.2 113.4 %all-gather.5.cloned.1.call-start = ((), (), s32[]{:S(2)}) async-start(), calls=%async_computation.3 | async-start | bytes 8650752 | tf_op jit(solution)/shard_map/all_gather | solution.py:32
  27.4 47.5 %copy-start.7 = (u32[256]{0:T(256)S(1)}, u32[256]{0:T(256)}, u32[]{:S(2)}) copy-start(u32[256]{0:T(256)} %constant.65) | copy-start | bytes 3076
  27.4 48.7 %copy-start.6 = (s32[64]{0:T(128)S(1)}, s32[64]{0:T(128)}, u32[]{:S(2)}) copy-start(s32[64]{0:T(128)} %param.9) | copy-start | bytes 772
  61.8 63.5 %copy-start.4 = (bf16[32,32,64]{2,0,1:T(8,128)(2,1)S(1)}, bf16[32,32,64]{2,0,1:T(8,128)(2,1)}, u32[]{:S(2)}) copy-start(bf16[32,32,64]{2,0,1:T(8,128)(2,1)} %copy.75) | copy-start | bytes 393220
  63.3 40.0 %all-to-all-start = ((f32[32,1,4096]{2,1,0:T(1,128)}), f32[32,1,4096]{2,1,0:T(1,128)S(1)}, u32[]{:S(2)}, u32[]{:S(2)}) async-start(f32[32,1,4096]{2,1,0:T(1,128)} %reshape.308), calls=%async_computation | async-start | bytes 1048576 | tf_op jit(solution)/shard_map/all_to_all | solution.py:47
  74.6 168.9 %all-gather.7.cloned.1.call-start = ((), (), s32[]{:S(2)}) async-start(), calls=%async_computation.4 | async-start | bytes 8650752 | tf_op jit(solution)/shard_map/all_gather | solution.py:32
  129.7 5.6 %copy-start.3 = (f32[64,32,64]{2,1,0:T(8,128)S(1)}, f32[64,32,64]{2,1,0:T(8,128)}, u32[]{:S(2)}) copy-start(f32[64,32,64]{2,1,0:T(8,128)} %reshape.309) | copy-start | bytes 1572868
  139.3 228.8 %all-gather.11.cloned.1.call-start = ((), (), s32[]{:S(2)}) async-start(), calls=%async_computation.6 | async-start | bytes 8650752 | tf_op jit(solution)/shard_map/all_gather | solution.py:32
  180.6 67.0 %copy-start.1 = (bf16[32,32,64]{2,1,0:T(8,128)(2,1)S(1)}, bf16[32,32,64]{2,1,0:T(8,128)(2,1)}, u32[]{:S(2)}) copy-start(bf16[32,32,64]{2,1,0:T(8,128)(2,1)} %fusion.32) | copy-start | bytes 393220
  270.1 45.5 %copy-start = (bf16[32,32,64]{2,1,0:T(8,128)(2,1)S(1)}, bf16[32,32,64]{2,1,0:T(8,128)(2,1)}, u32[]{:S(2)}) copy-start(bf16[32,32,64]{2,1,0:T(8,128)(2,1)} %fusion.33) | copy-start | bytes 393220
  308.2 30.7 %all-to-all-start.2 = ((f32[32,1,4096]{2,1,0:T(1,128)}), f32[32,1,4096]{2,1,0:T(1,128)S(1)}, u32[]{:S(2)}, u32[]{:S(2)}) async-start(f32[32,1,4096]{2,1,0:T(1,128)} %reshape.312), calls=%async_computation.2 | async-start | bytes 1048576 | tf_op jit(solution)/shard_map/all_to_all | solution.py:47
  315.3 78.2 %all-gather.9.cloned.1.call-start = ((), (), s32[]{:S(2)}) async-start(), calls=%async_computation.5 | async-start | bytes 1179648 | tf_op jit(solution)/shard_map/all_gather | solution.py:68
  375.5 5.6 %copy-start.2 = (f32[64,32,64]{2,1,0:T(8,128)S(1)}, f32[64,32,64]{2,1,0:T(8,128)}, u32[]{:S(2)}) copy-start(f32[64,32,64]{2,1,0:T(8,128)} %reshape.313) | copy-start | bytes 1572868
  375.5 18.1 %copy-start.5 = (bf16[32,2048]{1,0:T(8,128)(2,1)S(1)}, bf16[32,2048]{1,0:T(8,128)(2,1)}, u32[]{:S(2)}) copy-start(bf16[32,2048]{1,0:T(8,128)(2,1)} %reshape.182) | copy-start | bytes 393220
Sparse Core Ops, SparseCore 0:
  10.6 109.8 all-gather.4
  139.4 104.0 all-gather.6
  263.6 104.4 all-gather.10
  370.4 23.1 all-gather.8
where the time goes:
time: 549 us; the launch traced here: 546 us
  blocking collectives  199 us (36%)
  other arithmetic  127 us (23%)
  waiting for transfers between devices  97.1 us (18%)
  local copies, waits for them, and re-layouts  50.4 us (9%)
  matrix products  37.5 us (7%)
  starting transfers between devices  19 us (3%)
  between operations  14.8 us (3%)
    psum x1, blocking collectives, on_device(): lax.psum(partial_value.astype(jnp.bfloat16), 'row').astype(jnp.float32)  143 us
    scatter-add x3, other arithmetic, apply_operator(): jax.ops.segment_sum(mirror.reshape(rows_here * K, cols_here, B), flat_sou...  103 us
    all_gather x3, waiting for transfers between devices, apply_operator(): whole_blocks = lax.all_gather(block_vectors, 'row', axis=0, tiled=True)  65.9 us
    all_to_all x1, blocking collectives, apply_operator(): lax.all_to_all(spread[rows_here:], 'row', split_axis=0, concat_axis=0, ti...  30.1 us
    unnamed x1, blocking collectives  26.1 us
    all_to_all x2, waiting for transfers between devices, apply_operator(): lax.all_to_all(spread[rows_here:], 'row', split_axis=0, concat_axis=0, ti...  22.2 us
    dot_general x3, matrix products, apply_operator(): jnp.einsum('ima,ikab->ikmb', block_vectors, masked, preferred_element_typ...  19.2 us
    all_to_all x2, starting transfers between devices, apply_operator(): lax.all_to_all(spread[rows_here:], 'row', split_axis=0, concat_axis=0, ti...  18.4 us
  transfers between devices with their start and end apart: 6, of which 5 were waited for; matrix products, arithmetic and copies ran while one was open for 32% of the time, Pallas kernels for 0%

commit v1 on v0

--- a/solution.py
+++ b/solution.py
@@ -29,7 +29,9 @@
     )
 
     def apply_operator(block_vectors):
-        whole_blocks = lax.all_gather(block_vectors, "row", axis=0, tiled=True)
+        whole_blocks = jnp.concatenate(
+            lax.all_to_all(jnp.stack([block_vectors] * lax.axis_size("row")), "row", 0, 0), axis=0
+        )
         incoming = whole_blocks[global_rows]
         extended = jnp.concatenate([block_vectors, incoming], 0)
         picked = extended[flat_sources].reshape(rows_here, K, cols_here, B)

time: 549 us -> 800 us (1.46)
  local copies, waits for them, and re-layouts: 50.4 us -> 146 us
  waiting for transfers between devices: 97.1 us -> 177 us
  blocking collectives: 199 us -> 237 us
  starting transfers between devices: 19 us -> 55.6 us
    all_to_all x0 -> x3, waiting for transfers between devices: none -> 177 us  [apply_operator(): lax.all_to_all(jnp.stack([block_vectors] * lax.axis_size('row')), 'row',...]
    unnamed x26, local copies, waits for them, and re-layouts: 11.9 us -> 94 us
    unnamed x1, blocking collectives: 26.1 us -> 97.8 us
    all_gather x3 -> x0, waiting for transfers between devices: 65.9 us -> none  [apply_operator(): whole_blocks = lax.all_gather(block_vectors, 'row', axis=0, tiled=True)]
    all_to_all x1 -> x0, blocking collectives: 30.1 us -> none  [apply_operator(): lax.all_to_all(spread[rows_here:], 'row', split_axis=0, concat_axis=0, ti...]
    all_to_all x0 -> x3, starting transfers between devices: none -> 30.1 us  [apply_operator(): lax.all_to_all(jnp.stack([block_vectors] * lax.axis_size('row')), 'row',...]
    all_to_all x2 -> x3, waiting for transfers between devices: 22.2 us -> 0.01 us  [apply_operator(): lax.all_to_all(spread[rows_here:], 'row', split_axis=0, concat_axis=0, ti...]
    another operation x3 -> x6, local copies, waits for them, and re-layouts: 0.54 us -> 15.9 us  [the longest x3 15.3 us: apply_operator(): jnp.stack([block_vectors] * lax.axis_size('row'))]
  transfers between devices with their start and end apart: 6 -> 7, of which waited for: 5 -> 2; matrix products, arithmetic and copies ran while one was open for 32% -> 13% of each run, Pallas kernels for 0% -> 0%
where the time goes in v1:
time: 800 us; the launch traced here: 795 us
  blocking collectives  237 us (30%)
  waiting for transfers between devices  177 us (22%)
  local copies, waits for them, and re-layouts  146 us (18%)
  other arithmetic  126 us (16%)
  starting transfers between devices  55.6 us (7%)
  matrix products  37.6 us (5%)
  between operations  15.1 us (2%)
    all_to_all x3, waiting for transfers between devices, apply_operator(): lax.all_to_all(jnp.stack([block_vectors] * lax.axis_size('row')), 'row',...  177 us
    psum x1, blocking collectives, on_device(): lax.psum(partial_value.astype(jnp.bfloat16), 'row').astype(jnp.float32)  139 us
    scatter-add x3, other arithmetic, apply_operator(): jax.ops.segment_sum(mirror.reshape(rows_here * K, cols_here, B), flat_sou...  103 us
    unnamed x1, blocking collectives  97.8 us
    unnamed x26, local copies, waits for them, and re-layouts  94 us
    all_to_all x3, starting transfers between devices, apply_operator(): lax.all_to_all(jnp.stack([block_vectors] * lax.axis_size('row')), 'row',...  30.1 us
    all_to_all x3, starting transfers between devices, apply_operator(): lax.all_to_all(spread[rows_here:], 'row', split_axis=0, concat_axis=0, ti...  25.3 us
    dot_general x3, matrix products, apply_operator(): jnp.einsum('ima,ikab->ikmb', block_vectors, masked, preferred_element_typ...  19.3 us
  transfers between devices with their start and end apart: 7, of which 2 were waited for; matrix products, arithmetic and copies ran while one was open for 13% of the time, Pallas kernels for 0%

profile of v1, /device:TPU:16, one launch (start us, length us, event | category | flops | bytes accessed | tf_op | source)
XLA Modules:
  0.0 794.5 jit_solution(10956523127682627929)
XLA Ops:
  9.8 2.2 broadcast_select_fusion
  12.0 7.9 reshape.194
  19.9 6.4 fusion
  26.6 34.4 %scatter_fusion = f32[96,32,64]{2,1,0:T(8,128)S(1)} fusion(f32[96,32,64]{2,1,0:T(8,128)S(1)} %broadcast.200.clone, s32[384]{0:T(512)S(1)} %reshape.262, f32[384,32,64]{2,1,0:T(8,128)} %bitcast.77), kind=kCustom, calls=%fused_computation.7 | custom fusion | flops 786432 | bytes 9438720 | tf_op jit(solution)/shard_map/scatter-add | solution.py:44
  61.0 1.4 reshape.328
  62.5 11.3 %all-to-all-start.1 = ((f32[32,1,4096]{2,1,0:T(1,128)}), f32[32,1,4096]{2,1,0:T(1,128)S(1)}, u32[]{:S(2)}, u32[]{:S(2)}) async-start(f32[32,1,4096]{2,1,0:T(1,128)} %reshape.328), calls=%async_computation.1 | async-start | bytes 1048576 | tf_op jit(solution)/shard_map/all_to_all | solution.py:49
  73.9 5.1 stack.6
  79.0 13.9 %reshape.326 = bf16[32,2,32768]{2,1,0:T(2,128)(2,1)} reshape(bf16[32,32,32,64]{3,2,1,0:T(8,128)(2,1)} %stack.6) | data formatting | bytes 8388608
  92.9 10.0 %all-to-all-start = ((bf16[32,2,32768]{2,1,0:T(2,128)(2,1)}), bf16[32,2,32768]{2,1,0:T(2,128)(2,1)}, u32[]{:S(2)}, u32[]{:S(2)}) async-start(bf16[32,2,32768]{2,1,0:T(2,128)(2,1)} %reshape.326), calls=%async_computation | async-start | bytes 8388608 | tf_op jit(solution)/shard_map/all_to_all | solution.py:33
  104.6 97.8 %all-reduce = s32[2048]{0:T(1024)S(1)} all-reduce(s32[2048]{0:T(1024)S(1)} %dynamic-update-slice), channel_id=1, replica_groups=mesh['row'=32,'col'=8] {'row'}, use_global_device_ids=true, to_apply=%add | all-reduce | flops 2048 | bytes 16384
  203.8 1.9 reduce.2
  205.7 1.4 reshape.329
  207.1 13.6 %reshape.327 = bf16[32,32,32,64]{3,2,1,0:T(8,128)(2,1)} reshape(bf16[32,2,32768]{2,1,0:T(2,128)(2,1)} %all-to-all-done) | data formatting | bytes 8388608
  220.7 4.0 gather_fusion.1
  224.9 3.2 gather_fusion.2
  228.1 5.6 fusion.27
  233.7 3.2 scatter_fusion.1
  237.0 6.4 fusion.4
  243.6 34.4 %scatter_fusion.2 = f32[96,32,64]{2,1,0:T(8,128)S(1)} fusion(f32[96,32,64]{2,1,0:T(8,128)S(1)} %broadcast.200.clone.1, s32[384]{0:T(512)S(1)} %reshape.262, f32[384,32,64]{2,1,0:T(8,128)} %bitcast.78), kind=kCustom, calls=%fused_computation.9 | custom fusion | flops 786432 | bytes 9438720 | tf_op jit(solution)/shard_map/scatter-add | solution.py:44
  278.1 1.4 reshape.332
  279.5 7.5 all-to-all-start.3
  287.0 5.1 stack.7
  292.1 13.9 %reshape.330 = bf16[32,2,32768]{2,1,0:T(2,128)(2,1)} reshape(bf16[32,32,32,64]{3,2,1,0:T(8,128)(2,1)} %stack.7) | data formatting | bytes 8388608
  306.0 10.1 %all-to-all-start.2 = ((bf16[32,2,32768]{2,1,0:T(2,128)(2,1)}), bf16[32,2,32768]{2,1,0:T(2,128)(2,1)}, u32[]{:S(2)}, u32[]{:S(2)}) async-start(bf16[32,2,32768]{2,1,0:T(2,128)(2,1)} %reshape.330), calls=%async_computation.2 | async-start | bytes 8388608 | tf_op jit(solution)/shard_map/all_to_all | solution.py:33
  316.2 1.9 reduce.3
  318.1 1.4 reshape.333
  319.5 88.8 %all-to-all-done.2 = bf16[32,2,32768]{2,1,0:T(2,128)(2,1)} async-done(((bf16[32,2,32768]{2,1,0:T(2,128)(2,1)}), bf16[32,2,32768]{2,1,0:T(2,128)(2,1)}, u32[]{:S(2)}, u32[]{:S(2)}) %all-to-all-start.2) | async-done | bytes 4194336 | tf_op jit(solution)/shard_map/all_to_all | solution.py:33
  408.3 13.6 %reshape.331 = bf16[32,32,32,64]{3,2,1,0:T(8,128)(2,1)} reshape(bf16[32,2,32768]{2,1,0:T(2,128)(2,1)} %all-to-all-done.2) | data formatting | bytes 8388608
  421.9 4.8 gather_fusion.3
  427.9 3.2 gather_fusion.4
  431.1 5.5 fusion.24
  436.6 6.1 scatter_fusion.3
  442.9 6.4 fusion.8
  449.5 34.4 %scatter_fusion.4 = f32[96,32,64]{2,1,0:T(8,128)S(1)} fusion(f32[96,32,64]{2,1,0:T(8,128)S(1)} %broadcast.200, s32[384]{0:T(512)S(1)} %reshape.262, f32[384,32,64]{2,1,0:T(8,128)} %bitcast.76), kind=kCustom, calls=%fused_computation.11 | custom fusion | flops 786432 | bytes 9438720 | tf_op jit(solution)/shard_map/scatter-add | solution.py:44
  484.9 2.7 reshape.336
  487.6 6.5 all-to-all-start.5
  494.1 5.1 stack.8
  499.2 13.9 %reshape.334 = bf16[32,2,32768]{2,1,0:T(2,128)(2,1)} reshape(bf16[32,32,32,64]{3,2,1,0:T(8,128)(2,1)} %stack.8) | data formatting | bytes 8388608
  513.1 9.9 %all-to-all-start.4 = ((bf16[32,2,32768]{2,1,0:T(2,128)(2,1)}), bf16[32,2,32768]{2,1,0:T(2,128)(2,1)}, u32[]{:S(2)}, u32[]{:S(2)}) async-start(bf16[32,2,32768]{2,1,0:T(2,128)(2,1)} %reshape.334), calls=%async_computation.4 | async-start | bytes 8388608 | tf_op jit(solution)/shard_map/all_to_all | solution.py:33
  524.4 1.9 reduce.4
  527.7 88.3 %all-to-all-done.4 = bf16[32,2,32768]{2,1,0:T(2,128)(2,1)} async-done(((bf16[32,2,32768]{2,1,0:T(2,128)(2,1)}), bf16[32,2,32768]{2,1,0:T(2,128)(2,1)}, u32[]{:S(2)}, u32[]{:S(2)}) %all-to-all-start.4) | async-done | bytes 4194336 | tf_op jit(solution)/shard_map/all_to_all | solution.py:33
  616.0 13.6 %reshape.335 = bf16[32,32,32,64]{3,2,1,0:T(8,128)(2,1)} reshape(bf16[32,2,32768]{2,1,0:T(2,128)(2,1)} %all-to-all-done.4) | data formatting | bytes 8388608
  629.7 4.0 gather_fusion.5
  633.9 3.2 gather_fusion.6
  637.0 5.6 fusion.21
  642.6 3.2 scatter_fusion.5
  646.3 1.7 convolution_convert_fusion
  647.9 139.1 %psum.7 = bf16[256,2,32]{0,2,1:T(8,128)(2,1)S(1)} all-reduce(bf16[256,2,32]{0,2,1:T(8,128)(2,1)S(1)} %bitcast.88), channel_id=1, replica_groups=mesh['row'=32,'col'=8] {'row'}, use_global_device_ids=true, to_apply=%region_6.7 | all-reduce | flops 16384 | bytes 65536 | tf_op jit(solution)/shard_map/psum | solution.py:76
  (53 shorter events, 12.6 us)
Async XLA Ops:
  62.5 30.4 %all-to-all-start.1 = ((f32[32,1,4096]{2,1,0:T(1,128)}), f32[32,1,4096]{2,1,0:T(1,128)S(1)}, u32[]{:S(2)}, u32[]{:S(2)}) async-start(f32[32,1,4096]{2,1,0:T(1,128)} %reshape.328), calls=%async_computation.1 | async-start | bytes 1048576 | tf_op jit(solution)/shard_map/all_to_all | solution.py:49
  92.9 10.2 %copy-start.4 = (u32[256]{0:T(256)S(1)}, u32[256]{0:T(256)}, u32[]{:S(2)}) copy-start(u32[256]{0:T(256)} %constant.65) | copy-start | bytes 3076
  92.9 11.4 %copy-start.3 = (s32[64]{0:T(128)S(1)}, s32[64]{0:T(128)}, u32[]{:S(2)}) copy-start(s32[64]{0:T(128)} %param.9) | copy-start | bytes 772
  92.9 114.2 %all-to-all-start = ((bf16[32,2,32768]{2,1,0:T(2,128)(2,1)}), bf16[32,2,32768]{2,1,0:T(2,128)(2,1)}, u32[]{:S(2)}, u32[]{:S(2)}) async-start(bf16[32,2,32768]{2,1,0:T(2,128)(2,1)} %reshape.326), calls=%async_computation | async-start | bytes 8388608 | tf_op jit(solution)/shard_map/all_to_all | solution.py:33
  228.1 5.6 copy-start.1
  279.5 26.5 %all-to-all-start.3 = ((f32[32,1,4096]{2,1,0:T(1,128)}), f32[32,1,4096]{2,1,0:T(1,128)S(1)}, u32[]{:S(2)}, u32[]{:S(2)}) async-start(f32[32,1,4096]{2,1,0:T(1,128)} %reshape.332), calls=%async_computation.3 | async-start | bytes 1048576 | tf_op jit(solution)/shard_map/all_to_all | solution.py:49
  306.0 102.2 %all-to-all-start.2 = ((bf16[32,2,32768]{2,1,0:T(2,128)(2,1)}), bf16[32,2,32768]{2,1,0:T(2,128)(2,1)}, u32[]{:S(2)}, u32[]{:S(2)}) async-start(bf16[32,2,32768]{2,1,0:T(2,128)(2,1)} %reshape.330), calls=%async_computation.2 | async-start | bytes 8388608 | tf_op jit(solution)/shard_map/all_to_all | solution.py:33
  487.6 25.5 %all-to-all-start.5 = ((f32[32,1,4096]{2,1,0:T(1,128)}), f32[32,1,4096]{2,1,0:T(1,128)S(1)}, u32[]{:S(2)}, u32[]{:S(2)}) async-start(f32[32,1,4096]{2,1,0:T(1,128)} %reshape.336), calls=%async_computation.5 | async-start | bytes 1048576 | tf_op jit(solution)/shard_map/all_to_all | solution.py:49
  513.1 102.9 %all-to-all-start.4 = ((bf16[32,2,32768]{2,1,0:T(2,128)(2,1)}), bf16[32,2,32768]{2,1,0:T(2,128)(2,1)}, u32[]{:S(2)}, u32[]{:S(2)}) async-start(bf16[32,2,32768]{2,1,0:T(2,128)(2,1)} %reshape.334), calls=%async_computation.4 | async-start | bytes 8388608 | tf_op jit(solution)/shard_map/all_to_all | solution.py:33
  523.0 123.2 %all-gather.2.cloned.1.call-start = ((), (), s32[]{:S(2)}) async-start(), calls=%async_computation.6 | async-start | bytes 1179648 | tf_op jit(solution)/shard_map/all_gather | solution.py:70
  637.0 5.6 copy-start
  637.0 9.2 %copy-start.2 = (bf16[32,2048]{1,0:T(8,128)(2,1)S(1)}, bf16[32,2048]{1,0:T(8,128)(2,1)}, u32[]{:S(2)}) copy-start(bf16[32,2048]{1,0:T(8,128)(2,1)} %reshape.199) | copy-start | bytes 393220
Sparse Core Ops, SparseCore 0:
  526.3 25.6 all-gather.1
